TPU v7x, 32 devices: a whole 2x2x4 slice. The times are simulated.
32 devices in a mesh: seq: 16 (over z, y, x), tp: 2 (over core).
Axes of the slice: x: 2, y: 2, z: 4, core: 2. Of those that a mesh axis runs over, the one named last changes fastest.
Arguments:
- queries: bfloat16 [16, 32, 4096], P('seq', None, 'tp'), may hold values from -15 to 15
- tree_keys: bfloat16 [16, 32, 1024], P('seq', None, 'tp'), may hold values from -15 to 15
- tree_values: bfloat16 [16, 32, 1024], P('seq', None, 'tp'), may hold values from -6 to 6
- cache_keys: bfloat16 [9216, 1024], P('seq', 'tp'), may hold values from -15 to 15
- cache_values: bfloat16 [9216, 1024], P('seq', 'tp'), may hold values from -6 to 6
- residual: bfloat16 [16, 32, 4096], P('seq', None, 'tp'), may hold values from -6 to 6
- out_weight: bfloat16 [4096, 4096], P('tp'), may hold values from -0.125 to 0.125
- cache_len: int32 [16], replicated, may hold values from 88 to 1720, as said below
- parents: int32 [16, 32], P('seq'), may hold values from -1 to 30, as said below
- accept_rows: int32 [16, 8], P('seq'), may hold values from 0 to 31, as said below
- accept_len: int32 [16], replicated, may hold values from 1 to 8
Outputs:
- mixed: bfloat16 [16, 32, 4096], P('seq', None, 'tp')
- new_cache_keys: bfloat16 [9216, 1024], P('seq', 'tp')
- new_cache_values: bfloat16 [9216, 1024], P('seq', 'tp')
Inputs may be any that keep to these rules, and one draw needn't show every extreme that they name: Requests form aligned groups of 4 (requests 4 g to 4 g + 3). Request r owns cache_len[r] + 8 pool positions, these regions follow one another in request order from position 0, and the regions of one group fill exactly 2304 positions, so that group g's caches lie in pool positions 4 * 576 * g to 4 * 576 * (g + 1) - 1. parents[r, 0] = -1, and 0 <= parents[r, i] < i for i > 0. `accept_rows`: entries 0 to accept_len[r] - 1 are a chain of tree tokens that starts at token 0, each entry's parent being the entry before it; later entries are 31 and are not used.
All inputs are finite; a program needn't handle non-finite values.
Results may differ from a plain program's by a relative error of at most 0.009.
Values may be sent and summed in bfloat16 or wider, within the bound.
A program may use at most 64 MiB of HBM per device.

v0:
```python
import math

import jax
import jax.numpy as jnp
from jax import lax
from jax.sharding import PartitionSpec as P

HD = 128
TREE = 32
A_MAX = 8
GROUP = 4


NEG = -1e30


def partner_2(block, axis, stride):
    count = lax.axis_size(axis)
    route = []
    for low in range(count):
        high = low | 1 << stride
        if high != low and high < count:
            route += [(low, high), (high, low)]
    return lax.ppermute(block, axis, route)


def ancestry(parents):
    length = parents.shape[-1]
    members = jnp.arange(length, dtype=jnp.int32)
    ancestors = members[:, None] == members[None, :]
    current = parents
    for repeat in range(length - 1):
        ancestors = ancestors | (current[..., None] == members)
        hopped = jnp.take_along_axis(parents, jnp.maximum(current, 0), axis=-1)
        current = jnp.where(current >= 0, hopped, -1)
    return ancestors


def scale_heads(values, factors):
    return (values.reshape(factors.shape + (HD,)) * factors[..., None]).reshape(values.shape)


def combine(first_set, second_set):
    first_out, first_top, first_total = first_set
    second_out, second_top, second_total = second_set
    joint_top = jnp.maximum(first_top, second_top)
    first_factor = jnp.exp(first_top - joint_top)
    second_factor = jnp.exp(second_top - joint_top)
    joint_out = scale_heads(first_out, first_factor) + scale_heads(second_out, second_factor)
    return (joint_out, joint_top, first_total * first_factor + second_total * second_factor)


def on_device(
    queries,
    tree_keys,
    tree_values,
    cache_keys,
    cache_values,
    residual,
    out_weight,
    cache_len,
    parents,
    accept_rows,
    accept_len,
):
    seq_rank = lax.axis_index("seq")
    positions = cache_keys.shape[0]
    channels = cache_keys.shape[1]
    kv_local = channels // HD
    q_width = queries.shape[2]
    heads_local = q_width // HD
    sharing = heads_local // kv_local
    factor = 1.0 / math.sqrt(HD)
    regions = cache_len + A_MAX
    starts = jnp.cumsum(regions) - regions
    low_edge = seq_rank * positions
    places = low_edge + jnp.arange(positions, dtype=jnp.int32)
    keys_local = cache_keys.reshape(positions, kv_local, HD)
    values_local = cache_values.reshape(positions, kv_local, HD)
    tree_pair = jnp.concatenate([tree_keys[0], tree_values[0]], axis=-1)
    mine_rows = jnp.take(tree_pair, accept_rows[0], axis=0)[None]
    group_base = seq_rank // GROUP * GROUP
    levels = GROUP.bit_length() - 1
    gathered_q = queries
    for level in range(levels):
        partner = partner_2(gathered_q, "seq", level)
        upper_half = seq_rank // 2**level % 2 == 1
        gathered_q = jnp.where(
            upper_half,
            jnp.concatenate([partner, gathered_q], 0),
            jnp.concatenate([gathered_q, partner], 0),
        )
    number = gathered_q.shape[0]
    begin = lax.dynamic_slice_in_dim(starts, group_base, number)
    length = lax.dynamic_slice_in_dim(cache_len, group_base, number)
    inside = (places[None, :] >= begin[:, None]) & (places[None, :] < (begin + length)[:, None])
    shaped = gathered_q.reshape(number, TREE, kv_local, sharing, HD)
    scores = (
        jnp.einsum("rtkgd,pkd->rkgtp", shaped, keys_local, preferred_element_type=jnp.float32)
        * factor
    )
    valid = inside[:, None, None, None, :]
    top_score = jnp.max(jnp.where(valid, scores, NEG), axis=-1)
    raised = jnp.where(valid, jnp.exp(scores - top_score[..., None]), 0.0)
    total = jnp.sum(raised, axis=-1)
    summed = jnp.einsum(
        "rkgtp,pkd->rtkgd",
        raised.astype(jnp.bfloat16),
        values_local,
        preferred_element_type=jnp.float32,
    )
    top_rows = jnp.transpose(top_score, (0, 3, 1, 2)).reshape(number, TREE, heads_local)
    total_rows = jnp.transpose(total, (0, 3, 1, 2)).reshape(number, TREE, heads_local)
    partial_set = (summed.reshape(number, TREE, q_width), top_rows, total_rows)
    within = seq_rank - group_base
    for level in range(levels):
        partner_set = partner_2((partial_set[0], partial_set[1], partial_set[2]), "seq", level)
        partial_set = combine(partial_set, partner_set)
    cache_part = tuple((lax.dynamic_slice_in_dim(member, within, 1, 0) for member in partial_set))
    row_block = mine_rows
    for level in range(levels):
        partner_rows = partner_2(row_block, "seq", level)
        upper_half = seq_rank // 2**level % 2 == 1
        row_block = jnp.where(
            upper_half,
            jnp.concatenate([partner_rows, row_block], 0),
            jnp.concatenate([row_block, partner_rows], 0),
        )
    linked = ancestry(parents[0])
    shaped_q = queries[0].reshape(TREE, kv_local, sharing, HD)
    own_keys = tree_keys[0].reshape(TREE, kv_local, HD)
    own_values = tree_values[0].reshape(TREE, kv_local, HD)
    drafted = (
        jnp.einsum("tkgd,jkd->kgtj", shaped_q, own_keys, preferred_element_type=jnp.float32)
        * factor
    )
    tree_top = jnp.max(jnp.where(linked, drafted, NEG), axis=-1)
    tree_raised = jnp.where(linked, jnp.exp(drafted - tree_top[..., None]), 0.0)
    tree_total = jnp.sum(tree_raised, axis=-1)
    tree_out = jnp.einsum(
        "kgtj,jkd->tkgd",
        tree_raised.astype(jnp.bfloat16),
        own_values,
        preferred_element_type=jnp.float32,
    )
    tree_part = (
        tree_out.reshape(1, TREE, q_width),
        jnp.transpose(tree_top, (2, 0, 1)).reshape(1, TREE, heads_local),
        jnp.transpose(tree_total, (2, 0, 1)).reshape(1, TREE, heads_local),
    )
    joint_out, joint_top, joint_total = combine(cache_part, tree_part)
    attention = scale_heads(joint_out, 1.0 / joint_total).astype(jnp.bfloat16)[0]
    summed_heads = lax.psum_scatter(
        lax.dot_general(
            out_weight, attention, (((0,), (1,)), ((), ())), preferred_element_type=jnp.float32
        ).astype(jnp.bfloat16),
        "tp",
        scatter_dimension=0,
        tiled=True,
    ).astype(jnp.float32)
    mixed = (residual[0].astype(jnp.float32) + summed_heads.T).astype(jnp.bfloat16)[None]
    row_count = row_block.shape[0]
    row_begin = lax.dynamic_slice_in_dim(starts, group_base, row_count)
    row_length = lax.dynamic_slice_in_dim(cache_len, group_base, row_count)
    row_accepted = lax.dynamic_slice_in_dim(accept_len, group_base, row_count)
    column = jnp.arange(A_MAX, dtype=jnp.int32)
    targets = row_begin[:, None] + row_length[:, None] + column[None, :] - low_edge
    keep_row = (column[None, :] < row_accepted[:, None]) & (targets >= 0) & (targets < positions)
    targets = jnp.where(keep_row, targets, positions).reshape(-1)
    joined = jnp.concatenate([cache_keys, cache_values], axis=-1)
    joined = joined.at[targets].set(row_block.reshape(-1, 2 * channels), mode="drop")
    return (mixed, joined[:, :channels], joined[:, channels:])


def solution(mesh):
    return jax.shard_map(
        on_device,
        mesh=mesh,
        in_specs=(
            P("seq", None, "tp"),
            P("seq", None, "tp"),
            P("seq", None, "tp"),
            P("seq", "tp"),
            P("seq", "tp"),
            P("seq", None, "tp"),
            P("tp", None),
            P(),
            P("seq", None),
            P("seq", None),
            P(),
        ),
        out_specs=(P("seq", None, "tp"), P("seq", "tp"), P("seq", "tp")),
        check_vma=False,
    )
```

profile of v0, /device:TPU:0, one launch (start us, length us, event | category | flops | bytes accessed | tf_op | source)
XLA Modules:
  0.0 147.6 jit_solution(16349475866669061251)
XLA Ops:
  7.2 3.0 %collective-permute-start = (bf16[1,32,2048]{2,1,0:T(8,128)(2,1)}, bf16[1,32,2048]{2,1,0:T(8,128)(2,1)S(1)}, u32[]{:S(2)}, u32[]{:S(2)}) collective-permute-start(bf16[1,32,2048]{2,1,0:T(8,128)(2,1)} %param.13), channel_id=1, source_target_pairs={{0,2},{2,0},{4,6},{6,4},{8,10},{10,8},{12,14},{14,12},{16,18},{18,... | collective-permute-start | bytes 393224 | tf_op jit(solution)/shard_map/ppermute | solution.py:24
  11.6 0.8 pad_maximum_fusion.1
  15.8 1.4 gather_fusion.1
  17.9 1.4 gather_fusion.2
  19.2 1.4 gather_fusion.3
  20.6 1.4 gather_fusion.4
  22.0 1.4 gather_fusion.5
  23.4 1.4 gather_fusion.6
  24.8 1.4 gather_fusion.7
  26.1 1.4 gather_fusion.8
  27.5 1.4 gather_fusion.9
  28.9 0.7 gather_fusion.10
  29.7 0.7 gather_fusion.11
  30.4 0.7 gather_fusion.12
  31.1 0.7 gather_fusion.13
  31.9 0.7 gather_fusion.14
  33.3 0.7 gather_fusion.16
  34.0 0.7 gather_fusion.17
  34.8 0.7 gather_fusion.18
  45.0 2.1 %collective-permute-start.1 = (bf16[2,32,2048]{2,1,0:T(8,128)(2,1)S(1)}, bf16[2,32,2048]{2,1,0:T(8,128)(2,1)S(1)}, u32[]{:S(2)}, u32[]{:S(2)}) collective-permute-start(bf16[2,32,2048]{2,1,0:T(8,128)(2,1)S(1)} %maximum_select_fusion.2), channel_id=1, source_target_pairs={{0,4},{4,0},{2,6},{6,2},{8,12},{12,8},{10,14},{14,10},{16,20},{20,... | collective-permute-start | bytes 786440 | tf_op jit(solution)/shard_map/ppermute | solution.py:24
  47.3 5.5 %collective-permute-done.1 = bf16[2,32,2048]{2,1,0:T(8,128)(2,1)S(1)} collective-permute-done((bf16[2,32,2048]{2,1,0:T(8,128)(2,1)S(1)}, bf16[2,32,2048]{2,1,0:T(8,128)(2,1)S(1)}, u32[]{:S(2)}, u32[]{:S(2)}) %collective-permute-start.1) | collective-permute-done | bytes 262176 | tf_op jit(solution)/shard_map/ppermute | solution.py:24
  53.1 1.3 fusion
  54.3 2.3 %copy-done.1 = f32[4,4,32,4,576]{4,2,3,1,0:T(8,128)} copy-done((f32[4,4,32,4,576]{4,2,3,1,0:T(8,128)}, f32[4,4,32,4,576]{4,2,3,1,0:T(8,128)S(1)}, u32[]{:S(2)}) %copy-start.1) | copy-done | bytes 4718616
  56.7 1.2 fusion.12
  59.0 1.8 %collective-permute-start.3 = (f32[4,32,2048]{2,1,0:T(8,128)S(1)}, f32[4,32,2048]{2,1,0:T(8,128)}, u32[]{:S(2)}, u32[]{:S(2)}) collective-permute-start(f32[4,32,2048]{2,1,0:T(8,128)S(1)} %reshape_reshape.6), channel_id=1, source_target_pairs={{0,2},{2,0},{4,6},{6,4},{8,10},{10,8},{12,14},{14,12},{16,18},{18,... | collective-permute-start | bytes 3145736 | tf_op jit(solution)/shard_map/ppermute | solution.py:24
  61.1 3.5 %fusion.4 = f32[4,4,4,32]{3,2,0,1:T(4,128)S(1)} fusion(f32[4,4,32,4,576]{4,2,3,1,0:T(8,128)} %copy-done.1, f32[4,4,4,32]{3,2,0,1:T(4,128)S(1)} %get-tuple-element.77, pred[4,576]{1,0:T(4,128)(4,1)S(1)} %compare_and_fusion), kind=kLoop, calls=%fused_computation.39 | loop fusion | flops 4716544 | bytes 4737280 | tf_op jit(solution)/shard_map/reduce_sum | solution.py:105
  65.0 1.7 %collective-permute-start.2 = (f32[4,32,16]{1,2,0:T(8,128)S(1)}, f32[4,32,16]{1,2,0:T(8,128)S(1)}, u32[]{:S(2)}, u32[]{:S(2)}) collective-permute-start(f32[4,32,16]{1,2,0:T(8,128)S(1)} %bitcast.128), channel_id=1, source_target_pairs={{0,2},{2,0},{4,6},{6,4},{8,10},{10,8},{12,14},{14,12},{16,18},{18,... | collective-permute-start | bytes 24584 | tf_op jit(solution)/shard_map/ppermute | solution.py:24
  67.4 16.4 %collective-permute-done.6 = f32[4,32,16]{1,2,0:T(8,128)S(1)} collective-permute-done((f32[4,32,16]{1,2,0:T(8,128)S(1)}, f32[4,32,16]{1,2,0:T(8,128)S(1)}, u32[]{:S(2)}, u32[]{:S(2)}) %collective-permute-start.6) | collective-permute-done | bytes 8224 | tf_op jit(solution)/shard_map/ppermute | solution.py:24
  85.5 1.3 mul.148
  86.8 1.4 mul.149
  88.2 2.5 %multiply_add_fusion = f32[4,32,2048]{2,1,0:T(8,128)} fusion(f32[4,32,2048]{2,1,0:T(8,128)} %collective-permute-done.3, f32[4,32,2048]{2,1,0:T(8,128)S(1)} %mul.149, f32[4,32,2048]{2,1,0:T(8,128)S(1)} %reshape_reshape.6, f32[4,32,2048]{2,1,0:T(8,128)S(1)} %mul.146), kind=kLoop, calls=%fused_computation.51 | loop fusion | flops 786432 | bytes 5242880 | tf_op jit(solution)/shard_map/add | solution.py:49
  90.7 1.4 collective-permute-start.5
  94.1 1.3 sub.83
  96.0 1.4 collective-permute-start.7
  97.5 17.4 %collective-permute-done.4 = f32[4,32,16]{1,2,0:T(8,128)S(1)} collective-permute-done((f32[4,32,16]{1,2,0:T(8,128)}, f32[4,32,16]{1,2,0:T(8,128)S(1)}, u32[]{:S(2)}, u32[]{:S(2)}) %collective-permute-start.4) | collective-permute-done | bytes 8224 | tf_op jit(solution)/shard_map/ppermute | solution.py:24
  114.9 0.8 subtract_exponential_fusion.1
  116.9 0.8 fusion.91
  117.9 0.8 mul.162
  118.8 0.8 mul.166
  119.8 0.8 mul.176
  120.6 9.9 %fusion.3 = bf16[4096,32]{0,1:T(8,128)(2,1)} fusion(bf16[2048,4096]{1,0:T(8,128)(2,1)} %param.19, f32[1,32,2048]{2,1,0:T(8,128)} %mul.176, f32[1,32,2048]{2,1,0:T(8,128)} %mul.162, f32[4,32,2048]{2,1,0:T(8,128)S(1)} %mul.155, s32[]{:T(128)S(6)} %select_n.252, f32[4,32,2048]{2,1,0:T(8,128)} %collective-permute-done.5, f32[4,32,2048]{2,1,0:T(8,128)S(1)} %mul.152, ...), kind=kOutput, calls=%fused_computation.38 | convolution fusion | flops 537526272 | bytes 19136516 | tf_op jit(solution)/shard_map/dot_general | solution.py:154
  130.5 0.8 maximum_select_fusion.5
  131.3 1.2 collective-permute-start.9
  132.7 2.6 %collective-permute-done.9 = bf16[2,8,1024]{2,1,0:T(8,128)(2,1)S(1)} collective-permute-done((bf16[2,8,1024]{2,1,0:T(8,128)(2,1)S(1)}, bf16[2,8,1024]{2,1,0:T(8,128)(2,1)S(1)}, u32[]{:S(2)}, u32[]{:S(2)}) %collective-permute-start.9) | collective-permute-done | bytes 32800 | tf_op jit(solution)/shard_map/ppermute | solution.py:24
  135.3 1.4 scatter_custom_fusion
  136.8 1.1 fusion.99
  137.9 1.3 reduce-scatter.2.cloned.1.call-done
  139.2 1.6 %fusion.34 = bf16[1,32,2048]{2,1,0:T(8,128)(2,1)} fusion(bf16[2048,32]{0,1:T(8,128)(2,1)} %reduce-scatter.2.cloned.1.call-done, bf16[1,32,2048]{2,1,0:T(8,128)(2,1)S(1)} %copy-done.8), kind=kLoop, calls=%fused_computation.77 | loop fusion | flops 262144 | bytes 393216 | tf_op jit(solution)/shard_map/broadcast_in_dim | solution.py:161
  (176 shorter events, 25.0 us)
Async XLA Ops:
  7.2 21.7 %copy-start = (s32[1,32]{1,0:T(1,128)S(1)}, s32[1,32]{1,0:T(1,128)}, u32[]{:S(2)}) copy-start(s32[1,32]{1,0:T(1,128)} %param.21) | copy-start | bytes 388
  7.2 132.0 %reduce-scatter.2.cloned.1.call-start = ((), (), s32[]{:S(2)}) async-start(), calls=%async_computation.1 | async-start | bytes 393216 | tf_op jit(solution)/shard_map/reduce_scatter | solution.py:153
  7.2 37.7 %collective-permute-start = (bf16[1,32,2048]{2,1,0:T(8,128)(2,1)}, bf16[1,32,2048]{2,1,0:T(8,128)(2,1)S(1)}, u32[]{:S(2)}, u32[]{:S(2)}) collective-permute-start(bf16[1,32,2048]{2,1,0:T(8,128)(2,1)} %param.13), channel_id=1, source_target_pairs={{0,2},{2,0},{4,6},{6,4},{8,10},{10,8},{12,14},{14,12},{16,18},{18,... | collective-permute-start | bytes 393224 | tf_op jit(solution)/shard_map/ppermute | solution.py:24
  13.6 116.9 %collective-permute-start.8 = (bf16[1,8,1024]{2,1,0:T(8,128)(2,1)}, bf16[1,8,1024]{2,1,0:T(8,128)(2,1)}, u32[]{:S(2)}, u32[]{:S(2)}) collective-permute-start(bf16[1,8,1024]{2,1,0:T(8,128)(2,1)} %bitcast_select_fusion.1), channel_id=1, source_target_pairs={{0,2},{2,0},{4,6},{6,4},{8,10},{10,8},{12,14},{14,12},{16,18},{18,... | collective-permute-start | bytes 49160 | tf_op jit(solution)/shard_map/ppermute | solution.py:24
  29.6 14.6 %copy-start.12 = (s32[16]{0:T(128)S(1)}, s32[16]{0:T(128)}, u32[]{:S(2)}) copy-start(s32[16]{0:T(128)} %param.20) | copy-start | bytes 196
  30.4 14.0 %copy-start.6 = (bf16[1,32,2048]{2,1,0:T(8,128)(2,1)S(1)}, bf16[1,32,2048]{2,1,0:T(8,128)(2,1)}, u32[]{:S(2)}) copy-start(bf16[1,32,2048]{2,1,0:T(8,128)(2,1)} %param.13) | copy-start | bytes 393220
  31.1 13.4 %copy-start.9 = (bf16[1,32,512]{2,1,0:T(8,128)(2,1)S(1)}, bf16[1,32,512]{2,1,0:T(8,128)(2,1)}, u32[]{:S(2)}) copy-start(bf16[1,32,512]{2,1,0:T(8,128)(2,1)} %param.14) | copy-start | bytes 98308
  31.1 13.5 %copy-start.2 = (bf16[576,512]{1,0:T(8,128)(2,1)S(1)}, bf16[576,512]{1,0:T(8,128)(2,1)}, u32[]{:S(2)}) copy-start(bf16[576,512]{1,0:T(8,128)(2,1)} %param.16) | copy-start | bytes 1769476
  32.6 12.2 %copy-start.4 = (bf16[576,512]{1,0:T(8,128)(2,1)S(1)}, bf16[576,512]{1,0:T(8,128)(2,1)}, u32[]{:S(2)}) copy-start(bf16[576,512]{1,0:T(8,128)(2,1)} %param.17) | copy-start | bytes 1769476
  45.0 7.8 %collective-permute-start.1 = (bf16[2,32,2048]{2,1,0:T(8,128)(2,1)S(1)}, bf16[2,32,2048]{2,1,0:T(8,128)(2,1)S(1)}, u32[]{:S(2)}, u32[]{:S(2)}) collective-permute-start(bf16[2,32,2048]{2,1,0:T(8,128)(2,1)S(1)} %maximum_select_fusion.2), channel_id=1, source_target_pairs={{0,4},{4,0},{2,6},{6,2},{8,12},{12,8},{10,14},{14,10},{16,20},{20,... | collective-permute-start | bytes 786440 | tf_op jit(solution)/shard_map/ppermute | solution.py:24
  54.3 2.3 %copy-start.1 = (f32[4,4,32,4,576]{4,2,3,1,0:T(8,128)}, f32[4,4,32,4,576]{4,2,3,1,0:T(8,128)S(1)}, u32[]{:S(2)}) copy-start(f32[4,4,32,4,576]{4,2,3,1,0:T(8,128)S(1)} %get-tuple-element.78) | copy-start | bytes 14155780
  57.9 9.5 %copy-start.14 = (s32[16]{0:T(128)S(1)}, s32[16]{0:T(128)}, u32[]{:S(2)}) copy-start(s32[16]{0:T(128)} %param.23) | copy-start | bytes 196
  59.0 29.2 %collective-permute-start.3 = (f32[4,32,2048]{2,1,0:T(8,128)S(1)}, f32[4,32,2048]{2,1,0:T(8,128)}, u32[]{:S(2)}, u32[]{:S(2)}) collective-permute-start(f32[4,32,2048]{2,1,0:T(8,128)S(1)} %reshape_reshape.6), channel_id=1, source_target_pairs={{0,2},{2,0},{4,6},{6,4},{8,10},{10,8},{12,14},{14,12},{16,18},{18,... | collective-permute-start | bytes 3145736 | tf_op jit(solution)/shard_map/ppermute | solution.py:24
  64.6 19.2 %collective-permute-start.6 = (f32[4,32,16]{1,2,0:T(8,128)S(1)}, f32[4,32,16]{1,2,0:T(8,128)S(1)}, u32[]{:S(2)}, u32[]{:S(2)}) collective-permute-start(f32[4,32,16]{1,2,0:T(8,128)S(1)} %bitcast.126), channel_id=1, source_target_pairs={{0,2},{2,0},{4,6},{6,4},{8,10},{10,8},{12,14},{14,12},{16,18},{18,... | collective-permute-start | bytes 24584 | tf_op jit(solution)/shard_map/ppermute | solution.py:24
  65.0 19.2 %collective-permute-start.2 = (f32[4,32,16]{1,2,0:T(8,128)S(1)}, f32[4,32,16]{1,2,0:T(8,128)S(1)}, u32[]{:S(2)}, u32[]{:S(2)}) collective-permute-start(f32[4,32,16]{1,2,0:T(8,128)S(1)} %bitcast.128), channel_id=1, source_target_pairs={{0,2},{2,0},{4,6},{6,4},{8,10},{10,8},{12,14},{14,12},{16,18},{18,... | collective-permute-start | bytes 24584 | tf_op jit(solution)/shard_map/ppermute | solution.py:24
  85.2 7.0 %copy-start.10 = (bf16[1,32,512]{2,1,0:T(8,128)(2,1)S(1)}, bf16[1,32,512]{2,1,0:T(8,128)(2,1)}, u32[]{:S(2)}) copy-start(bf16[1,32,512]{2,1,0:T(8,128)(2,1)} %param.15) | copy-start | bytes 98308
  90.7 29.8 %collective-permute-start.5 = (f32[4,32,2048]{2,1,0:T(8,128)}, f32[4,32,2048]{2,1,0:T(8,128)}, u32[]{:S(2)}, u32[]{:S(2)}) collective-permute-start(f32[4,32,2048]{2,1,0:T(8,128)} %multiply_add_fusion), channel_id=1, source_target_pairs={{0,4},{4,0},{2,6},{6,2},{8,12},{12,8},{10,14},{14,10},{16,20},{20,... | collective-permute-start | bytes 3145736 | tf_op jit(solution)/shard_map/ppermute | solution.py:24
  92.5 22.4 %collective-permute-start.4 = (f32[4,32,16]{1,2,0:T(8,128)}, f32[4,32,16]{1,2,0:T(8,128)S(1)}, u32[]{:S(2)}, u32[]{:S(2)}) collective-permute-start(f32[4,32,16]{1,2,0:T(8,128)} %get-tuple-element.67), channel_id=1, source_target_pairs={{0,4},{4,0},{2,6},{6,2},{8,12},{12,8},{10,14},{14,10},{16,20},{20,... | collective-permute-start | bytes 24584 | tf_op jit(solution)/shard_map/ppermute | solution.py:24
  93.8 23.1 %copy-start.11 = (f32[4,4,32]{2,1,0:T(4,128)S(1)}, f32[4,4,32]{2,1,0:T(4,128)}, u32[]{:S(2)}) copy-start(f32[4,4,32]{2,1,0:T(4,128)} %fusion.31) | copy-start | bytes 6148
  96.0 20.8 %collective-permute-start.7 = (f32[4,32,16]{1,2,0:T(8,128)}, f32[4,32,16]{1,2,0:T(8,128)}, u32[]{:S(2)}, u32[]{:S(2)}) collective-permute-start(f32[4,32,16]{1,2,0:T(8,128)} %get-tuple-element.64), channel_id=1, source_target_pairs={{0,4},{4,0},{2,6},{6,2},{8,12},{12,8},{10,14},{14,10},{16,20},{20,... | collective-permute-start | bytes 24584 | tf_op jit(solution)/shard_map/ppermute | solution.py:24
  115.7 0.7 copy-start.7
  120.5 9.9 %copy-start.13 = (s32[32,1]{0,1:T(1,128)S(1)}, s32[32,1]{0,1:T(1,128)}, u32[]{:S(2)}) copy-start(s32[32,1]{0,1:T(1,128)} %sub.83) | copy-start | bytes 388
  120.5 10.0 %copy-start.15 = (pred[32,1]{0,1:T(4,128)(4,1)S(1)}, pred[32,1]{0,1:T(4,128)(4,1)}, u32[]{:S(2)}) copy-start(pred[32,1]{0,1:T(4,128)(4,1)} %lt.121) | copy-start | bytes 100
  120.5 12.0 %copy-start.3 = (bf16[576,512]{1,0:T(8,128)(2,1)S(1)}, bf16[576,512]{1,0:T(8,128)(2,1)}, u32[]{:S(2)}) copy-start(bf16[576,512]{1,0:T(8,128)(2,1)} %param.16) | copy-start | bytes 1769476
  120.5 12.0 %copy-start.5 = (bf16[576,512]{1,0:T(8,128)(2,1)S(1)}, bf16[576,512]{1,0:T(8,128)(2,1)}, u32[]{:S(2)}) copy-start(bf16[576,512]{1,0:T(8,128)(2,1)} %param.17) | copy-start | bytes 1769476
  130.5 8.7 %copy-start.8 = (bf16[1,32,2048]{2,1,0:T(8,128)(2,1)S(1)}, bf16[1,32,2048]{2,1,0:T(8,128)(2,1)}, u32[]{:S(2)}) copy-start(bf16[1,32,2048]{2,1,0:T(8,128)(2,1)} %param.18) | copy-start | bytes 393220
  131.3 4.0 %collective-permute-start.9 = (bf16[2,8,1024]{2,1,0:T(8,128)(2,1)S(1)}, bf16[2,8,1024]{2,1,0:T(8,128)(2,1)S(1)}, u32[]{:S(2)}, u32[]{:S(2)}) collective-permute-start(bf16[2,8,1024]{2,1,0:T(8,128)(2,1)S(1)} %maximum_select_fusion.5), channel_id=1, source_target_pairs={{0,4},{4,0},{2,6},{6,2},{8,12},{12,8},{10,14},{14,10},{16,20},{20,... | collective-permute-start | bytes 98312 | tf_op jit(solution)/shard_map/ppermute | solution.py:24
Sparse Core Ops, SparseCore 0:
  130.6 8.5 reduce-scatter.1
where the time goes:
time: 148 us
  waiting for transfers between devices  43.6 us (29%)
  local copies, waits for them, and re-layouts  42.6 us (29%)
  other arithmetic  19.9 us (13%)
  between operations  14.8 us (10%)
  starting transfers between devices  13.8 us (9%)
  matrix products  12.9 us (9%)
    ppermute x10, waiting for transfers between devices, partner_2(): return lax.ppermute(block, axis, route)  42.3 us
    gather x30, local copies, waits for them, and re-layouts, ancestry(): hopped = jnp.take_along_axis(parents, jnp.maximum(current, 0), axis=-1)  26.8 us
    ppermute x10, starting transfers between devices, partner_2(): return lax.ppermute(block, axis, route)  13.7 us
    dot_general x1, matrix products, on_device(): lax.dot_general(out_weight, attention, (((0,), (1,)), ((), ())), preferre...  9.89 us
    mul x17, local copies, waits for them, and re-layouts, scale_heads(): values.reshape(factors.shape + (HD,)) * factors[..., None]  7.08 us
    reduce_sum x1, other arithmetic, on_device(): total = jnp.sum(raised, axis=-1)  3.46 us
  transfers between devices with their start and end apart: 11, of which 6 were waited for; matrix products, arithmetic and copies ran while one was open for 48% of the time, Pallas kernels for 0%

commit v1 on v0

v1 whole, which is shorter than its diff:
```python
import functools
import math

import jax
import jax.numpy as jnp
from jax import lax
from jax.experimental import pallas as pl
from jax.experimental.pallas import tpu as pltpu
from jax.sharding import PartitionSpec as P

HD = 128
TREE = 32
A_MAX = 8
GROUP = 4
NEG = -1e30
FLOOR = -1e29
TAIL = 16
MESH = pl.DeviceIdType.MESH


def kernel(
    n_tp,
    len_ref,
    acc_len_ref,
    parents_ref,
    accept_ref,
    q_hbm,
    tk_hbm,
    tv_hbm,
    ck_hbm,
    cv_hbm,
    res_hbm,
    w_hbm,
    mixed_ref,
    nk_hbm,
    nv_hbm,
    kbuf,
    vbuf,
    vt,
    qown,
    qbuf,
    bias,
    own_o,
    own_s,
    psend,
    precv,
    rows,
    rrecv,
    wbuf,
    att,
    acc,
    tsend,
    trecv,
    resbuf,
    nk,
    nv,
    loc_sem,
    w_sem,
    out_sem,
    q_ss,
    q_rs,
    p_ss,
    p_rs,
    r_ss,
    r_rs,
    t_ss,
    t_rs,
):
    positions, channels = ck_hbm.shape
    kv = channels // HD
    qk = q_hbm.shape[2] // kv
    sharing = qk // HD
    lanes = sharing * TREE
    span = kbuf.shape[0]
    used = positions + TREE
    w_loc = res_hbm.shape[2]
    scale = math.log2(math.e) / math.sqrt(HD)

    seq = lax.axis_index("seq")
    tp = lax.axis_index("tp")
    base = seq // GROUP * GROUP
    within = seq - base
    low, high = within % 2, within // 2

    def peer_of(d):
        return (low + d % 2) % 2 + 2 * ((high + d // 2) % 2)

    locals_ = [
        pltpu.make_async_copy(tk_hbm.at[0], kbuf.at[pl.ds(positions, TREE)], loc_sem.at[0]),
        pltpu.make_async_copy(tv_hbm.at[0], vbuf.at[pl.ds(positions, TREE)], loc_sem.at[1]),
        pltpu.make_async_copy(q_hbm.at[0], qown, loc_sem.at[2]),
        pltpu.make_async_copy(ck_hbm, kbuf.at[pl.ds(0, positions)], loc_sem.at[3]),
        pltpu.make_async_copy(cv_hbm, vbuf.at[pl.ds(0, positions)], loc_sem.at[4]),
        pltpu.make_async_copy(res_hbm.at[0], resbuf, loc_sem.at[5]),
    ]
    for c in locals_:
        c.start()

    barrier = pltpu.get_barrier_semaphore()
    for d in range(1, GROUP):
        pl.semaphore_signal(barrier, inc=1, device_id=(base + peer_of(d), tp), device_id_type=MESH)
    for d in range(1, n_tp):
        pl.semaphore_signal(barrier, inc=1, device_id=(seq, (tp + d) % n_tp), device_id_type=MESH)
    pl.semaphore_wait(barrier, GROUP - 1 + n_tp - 1)

    def q_copy(d, k):
        return pltpu.make_async_remote_copy(
            src_ref=q_hbm.at[0, :, pl.ds(pl.multiple_of(k * qk, qk), qk)],
            dst_ref=qbuf.at[d - 1, k],
            send_sem=q_ss.at[d - 1, k],
            recv_sem=q_rs.at[d - 1, k],
            device_id=(base + peer_of(d), tp),
            device_id_type=MESH,
        )

    def p_copy(d, k):
        return pltpu.make_async_remote_copy(
            src_ref=psend.at[d - 1, k],
            dst_ref=precv.at[d - 1, k],
            send_sem=p_ss.at[d - 1, k],
            recv_sem=p_rs.at[d - 1, k],
            device_id=(base + peer_of(d), tp),
            device_id_type=MESH,
        )

    def r_copy(d):
        return pltpu.make_async_remote_copy(
            src_ref=rows,
            dst_ref=rrecv.at[d - 1],
            send_sem=r_ss.at[d - 1],
            recv_sem=r_rs.at[d - 1],
            device_id=(base + peer_of(d), tp),
            device_id_type=MESH,
        )

    def t_copy(d):
        return pltpu.make_async_remote_copy(
            src_ref=tsend.at[d - 1],
            dst_ref=trecv.at[d - 1],
            send_sem=t_ss.at[d - 1],
            recv_sem=t_rs.at[d - 1],
            device_id=(seq, (tp + d) % n_tp),
            device_id_type=MESH,
        )

    def w_copy(k):
        rows_k = pl.ds(pl.multiple_of(k * qk, qk), qk)
        return pltpu.make_async_copy(w_hbm.at[rows_k], wbuf.at[rows_k], w_sem.at[k])

    for k in range(kv):
        for d in (1, 2, 3):
            q_copy(d, k).start()
    for k in range(kv):
        w_copy(k).start()

    lens = [len_ref[base + r] for r in range(GROUP)]
    begins = []
    at = -within * positions
    for r in range(GROUP):
        begins.append(at)
        at = at + lens[r] + A_MAX
    place = lax.broadcasted_iota(jnp.int32, (positions, lanes), 0)
    for d in range(GROUP):
        peer = peer_of(d)
        first, size = begins[0], lens[0]
        for r in range(1, GROUP):
            first = jnp.where(peer == r, begins[r], first)
            size = jnp.where(peer == r, lens[r], size)
        inside = (place >= first) & (place < first + size)
        bias[d, pl.ds(0, positions), :] = jnp.where(inside, 0.0, NEG)
        bias[d, pl.ds(positions, span - positions), :] = jnp.full(
            (span - positions, lanes), NEG, jnp.float32
        )

    i32 = jnp.int32
    row_i = lax.broadcasted_iota(i32, (TREE, TREE), 0)
    col_i = lax.broadcasted_iota(i32, (TREE, TREE), 1)
    parents = jnp.broadcast_to(parents_ref[...], (TREE, TREE))
    reach = jnp.where((row_i == col_i) | (parents == row_i), 1.0, 0.0)
    for _ in range((TREE - 1).bit_length()):
        half = reach.astype(jnp.bfloat16)
        reach = jnp.minimum(jnp.dot(half, half, preferred_element_type=jnp.float32), 1.0)
    spread = jnp.where(
        lax.broadcasted_iota(i32, (TREE, lanes), 0)
        == lax.broadcasted_iota(i32, (TREE, lanes), 1) % TREE,
        1.0,
        0.0,
    ).astype(jnp.bfloat16)
    linked = jnp.dot(reach.astype(jnp.bfloat16), spread, preferred_element_type=jnp.float32)
    bias[0, pl.ds(positions, TREE), :] = jnp.where(linked > 0.5, 0.0, NEG)

    if span > used:
        kbuf[pl.ds(used, span - used), :] = jnp.zeros((span - used, channels), jnp.bfloat16)
        vbuf[pl.ds(used, span - used), :] = jnp.zeros((span - used, channels), jnp.bfloat16)

    locals_[0].wait()
    locals_[1].wait()
    chosen = jnp.where(
        jnp.broadcast_to(accept_ref[...], (TREE, A_MAX))
        == lax.broadcasted_iota(i32, (TREE, A_MAX), 0),
        1.0,
        0.0,
    ).astype(jnp.bfloat16)
    dims = (((0,), (0,)), ((), ()))
    tree_rows = pl.ds(positions, TREE)
    rows[...] = jnp.concatenate(
        [
            lax.dot_general(chosen, kbuf[tree_rows, :], dims, preferred_element_type=jnp.float32),
            lax.dot_general(chosen, vbuf[tree_rows, :], dims, preferred_element_type=jnp.float32),
        ],
        axis=0,
    ).astype(jnp.bfloat16)
    for d in range(1, GROUP):
        r_copy(d).start()

    for i in (2, 3, 4):
        locals_[i].wait()
    for k in range(kv):
        vt[k] = vbuf[:, k * HD : (k + 1) * HD].astype(jnp.float32).T.astype(jnp.bfloat16)

    def attend(queries, k, which):
        stacked = jnp.concatenate(
            [queries[:, g * HD : (g + 1) * HD] for g in range(sharing)], axis=0
        )
        keys = kbuf[:, pl.ds(pl.multiple_of(k * HD, HD), HD)]
        scores = lax.dot_general(
            keys, stacked, (((1,), (1,)), ((), ())), preferred_element_type=jnp.float32
        )
        scores = scores + bias[which]
        top = jnp.maximum(jnp.max(scores, axis=0, keepdims=True), FLOOR)
        top = top.astype(jnp.bfloat16).astype(jnp.float32)
        raised = jnp.exp2((scores - top) * scale)
        total = jnp.sum(raised, axis=0, keepdims=True)
        out = jnp.dot(vt[k], raised.astype(jnp.bfloat16), preferred_element_type=jnp.float32)
        return out, top, total

    def own_step(k, carry):
        out, top, total = attend(qown[:, pl.ds(pl.multiple_of(k * qk, qk), qk)], k, 0)
        own_o[k] = out
        own_s[k] = jnp.concatenate(
            [top, total, jnp.zeros((6, lanes), jnp.float32)], axis=0
        )
        return carry

    lax.fori_loop(0, kv, own_step, 0)

    tail_row = lax.broadcasted_iota(i32, (TAIL, lanes), 0)

    def peer_step(k, carry):
        for d in (1, 2, 3):
            q_copy(d, k).wait_recv()
            out, top, total = attend(qbuf[d - 1, k], k, d)
            psend[d - 1, k, pl.ds(0, HD), :] = out.astype(jnp.bfloat16)
            main = total.astype(jnp.bfloat16).astype(jnp.float32)
            tail = jnp.where(
                tail_row == 0, top, jnp.where(tail_row == 1, main, total - main)
            )
            psend[d - 1, k, pl.ds(HD, TAIL), :] = tail.astype(jnp.bfloat16)
            p_copy(d, k).start()
        return carry

    lax.fori_loop(0, kv, peer_step, 0)

    for d in range(1, GROUP):
        r_copy(d).wait_recv()
    wide = GROUP * 2 * A_MAX
    col = lax.broadcasted_iota(i32, (1, wide), 1)
    slot = col % (2 * A_MAX)
    targets = jnp.full((1, wide), -1, i32)
    for d in range(GROUP):
        peer = peer_of(d)
        end, taken = begins[0] + lens[0], acc_len_ref[base]
        for r in range(1, GROUP):
            end = jnp.where(peer == r, begins[r] + lens[r], end)
            taken = jnp.where(peer == r, acc_len_ref[base + r], taken)
        hit = (col // (2 * A_MAX) == d) & (slot % A_MAX < taken)
        targets = jnp.where(hit, end + slot % A_MAX, targets)
    arrived = jnp.concatenate([rows[...]] + [rrecv[d] for d in range(GROUP - 1)], axis=0)
    where_row = lax.broadcasted_iota(i32, (positions, wide), 0)
    outs = []
    for half, (old, new, dest) in enumerate(((kbuf, nk, nk_hbm), (vbuf, nv, nv_hbm))):
        mine = jnp.where(slot // A_MAX == half, targets, -1)
        pick = jnp.where(where_row == mine, 1.0, 0.0)
        changed = jnp.max(pick, axis=1, keepdims=True)
        put = jnp.dot(pick.astype(jnp.bfloat16), arrived, preferred_element_type=jnp.float32)
        new[...] = jnp.where(changed > 0.5, put, old[pl.ds(0, positions), :].astype(jnp.float32)).astype(
            jnp.bfloat16
        )
        copy = pltpu.make_async_copy(new, dest, out_sem.at[half])
        copy.start()
        outs.append(copy)

    def gather(k):
        tops = [own_s[k, pl.ds(0, 1), :]]
        totals = [own_s[k, pl.ds(1, 1), :]]
        parts = [own_o[k]]
        for d in (1, 2, 3):
            p_copy(d, k).wait_recv()
            tail = precv[d - 1, k, pl.ds(HD, TAIL), :].astype(jnp.float32)
            tops.append(tail[0:1])
            totals.append(tail[1:2] + tail[2:3])
            parts.append(precv[d - 1, k, pl.ds(0, HD), :].astype(jnp.float32))
        top = functools.reduce(jnp.maximum, tops)
        factors = [jnp.exp2((t - top) * scale) for t in tops]
        total = sum(f * t for f, t in zip(factors, totals))
        out = sum(f * p for f, p in zip(factors, parts)) * (1.0 / total)
        turned = out.T.astype(jnp.bfloat16)
        for g in range(sharing):
            att[:, g * HD : (g + 1) * HD] = turned[g * TREE : (g + 1) * TREE]

    step = min(w_loc, 1024)

    def project(k, d):
        peer = (tp + d) % n_tp
        left = att[...]
        for c in range(w_loc // step):
            columns = pl.ds(pl.multiple_of(peer * w_loc + c * step, HD), step)
            part = jnp.dot(
                left,
                wbuf[pl.ds(pl.multiple_of(k * qk, qk), qk), columns],
                preferred_element_type=jnp.float32,
            )
            acc[d, :, c * step : (c + 1) * step] += part

    acc[...] = jnp.zeros_like(acc)

    def out_step(k, carry):
        w_copy(k).wait()
        gather(k)
        for d in range(n_tp):
            project(k, d)
        return carry

    lax.fori_loop(0, kv - 1, out_step, 0)
    w_copy(kv - 1).wait()
    gather(kv - 1)
    for d in range(1, n_tp):
        project(kv - 1, d)
        tsend[d - 1] = acc[d].astype(jnp.bfloat16)
        t_copy(d).start()
    project(kv - 1, 0)
    locals_[5].wait()
    result = acc[0] + resbuf[...].astype(jnp.float32)
    for d in range(1, n_tp):
        t_copy(d).wait_recv()
        result = result + trecv[d - 1].astype(jnp.float32)
    mixed_ref[0] = result.astype(jnp.bfloat16)

    for copy in outs:
        copy.wait()
    for d in range(1, GROUP):
        r_copy(d).wait_send()
        for k in range(kv):
            q_copy(d, k).wait_send()
            p_copy(d, k).wait_send()
    for d in range(1, n_tp):
        t_copy(d).wait_send()


def on_device(n_tp, queries, tree_keys, tree_values, cache_keys, cache_values, residual, out_weight, cache_len, parents, accept_rows, accept_len):
    positions, channels = cache_keys.shape
    kv = channels // HD
    q_width = queries.shape[2]
    qk = q_width // kv
    lanes = qk // HD * TREE
    w_loc = residual.shape[2]
    span = -(-(positions + TREE) // 128) * 128
    bf16, f32 = jnp.bfloat16, jnp.float32
    peers = GROUP - 1
    vmem = pltpu.VMEM
    dma = pltpu.SemaphoreType.DMA
    hbm = pl.BlockSpec(memory_space=pl.ANY)
    smem = pl.BlockSpec(memory_space=pltpu.SMEM)
    local = pl.BlockSpec(memory_space=pltpu.VMEM)
    return pl.pallas_call(
        functools.partial(kernel, n_tp),
        out_shape=(
            jax.ShapeDtypeStruct(residual.shape, bf16),
            jax.ShapeDtypeStruct(cache_keys.shape, bf16),
            jax.ShapeDtypeStruct(cache_values.shape, bf16),
        ),
        in_specs=[smem, smem, local, local] + [hbm] * 7,
        out_specs=(local, hbm, hbm),
        scratch_shapes=[
            vmem((span, channels), bf16),
            vmem((span, channels), bf16),
            vmem((kv, HD, span), bf16),
            vmem((TREE, q_width), bf16),
            vmem((peers, kv, TREE, qk), bf16),
            vmem((GROUP, span, lanes), f32),
            vmem((kv, HD, lanes), f32),
            vmem((kv, 8, lanes), f32),
            vmem((peers, kv, HD + TAIL, lanes), bf16),
            vmem((peers, kv, HD + TAIL, lanes), bf16),
            vmem((2 * A_MAX, channels), bf16),
            vmem((peers, 2 * A_MAX, channels), bf16),
            vmem(out_weight.shape, bf16),
            vmem((TREE, qk), bf16),
            vmem((n_tp, TREE, w_loc), f32),
            vmem((max(n_tp - 1, 1), TREE, w_loc), bf16),
            vmem((max(n_tp - 1, 1), TREE, w_loc), bf16),
            vmem((TREE, w_loc), bf16),
            vmem((positions, channels), bf16),
            vmem((positions, channels), bf16),
            dma((6,)),
            dma((kv,)),
            dma((2,)),
            dma((peers, kv)),
            dma((peers, kv)),
            dma((peers, kv)),
            dma((peers, kv)),
            dma((peers,)),
            dma((peers,)),
            dma((max(n_tp - 1, 1),)),
            dma((max(n_tp - 1, 1),)),
        ],
        compiler_params=pltpu.CompilerParams(
            collective_id=0, has_side_effects=True, vmem_limit_bytes=48 * 1024 * 1024
        ),
        name="tree_attention",
    )(cache_len, accept_len, parents, accept_rows, queries, tree_keys, tree_values, cache_keys, cache_values, residual, out_weight)


def solution(mesh):
    return jax.shard_map(
        functools.partial(on_device, mesh.shape["tp"]),
        mesh=mesh,
        in_specs=(
            P("seq", None, "tp"),
            P("seq", None, "tp"),
            P("seq", None, "tp"),
            P("seq", "tp"),
            P("seq", "tp"),
            P("seq", None, "tp"),
            P("tp", None),
            P(),
            P("seq", None),
            P("seq", None),
            P(),
        ),
        out_specs=(P("seq", None, "tp"), P("seq", "tp"), P("seq", "tp")),
        check_vma=False,
    )
```

time: 148 us -> 32.7 us (0.22)
  waiting for transfers between devices: 43.6 us -> 0 us
  local copies, waits for them, and re-layouts: 42.6 us -> 10.3 us
  Pallas kernels: 0 us -> 21.3 us
  other arithmetic: 19.9 us -> 0 us
  between operations: 14.8 us -> 0.66 us
  starting transfers between devices: 13.8 us -> 0 us
  matrix products: 12.9 us -> 0 us
    ppermute x10 -> x0, waiting for transfers between devices: 42.3 us -> none  [partner_2(): return lax.ppermute(block, axis, route)]
    gather x31 -> x0, local copies, waits for them, and re-layouts: 27.4 us -> none  [the longest x30 26.8 us: ancestry(): hopped = jnp.take_along_axis(parents, jnp.maximum(current, 0), axis=-1)]
    pallas_call x0 -> x1, Pallas kernels: none -> 21.3 us  [on_device(): pl.pallas_call(functools.partial(kernel, n_tp), out_shape=(jax.ShapeDtype...]
    ppermute x10 -> x0, starting transfers between devices: 13.7 us -> none  [partner_2(): return lax.ppermute(block, axis, route)]
    dot_general x5 -> x0, matrix products: 12.9 us -> none  [the longest x1 9.89 us: on_device(): lax.dot_general(out_weight, attention, (((0,), (1,)), ((), ())), preferre...]
    unnamed x32 -> x23, local copies, waits for them, and re-layouts: 2.39 us -> 10.3 us
    mul x17 -> x0, local copies, waits for them, and re-layouts: 7.08 us -> none  [scale_heads(): values.reshape(factors.shape + (HD,)) * factors[..., None]]
    reduce_sum x2 -> x0, other arithmetic: 4.14 us -> none  [the longest x1 3.46 us: on_device(): total = jnp.sum(raised, axis=-1)]
  transfers between devices with their start and end apart: 11 -> 0, of which waited for: 6 -> 0; matrix products, arithmetic and copies ran while one was open for 48% -> 0% of each run, Pallas kernels for 0% -> 0%
where the time goes in v1:
time: 32.7 us; the launch traced here: 32.3 us
  Pallas kernels  21.3 us (65%)
  local copies, waits for them, and re-layouts  10.3 us (31%)
  between operations  0.66 us (2%)
    pallas_call x1, Pallas kernels, on_device(): pl.pallas_call(functools.partial(kernel, n_tp), out_shape=(jax.ShapeDtype...  21.3 us
    unnamed x23, local copies, waits for them, and re-layouts  10.3 us

profile of v1, /device:TPU:0, one launch (start us, length us, event | category | flops | bytes accessed | tf_op | source)
XLA Modules:
  0.0 32.3 jit_solution(7763729233841318992)
XLA Ops:
  0.6 0.0 copy-start
  0.6 1.1 %copy-done = bf16[576,512]{1,0:T(8,128)(2,1)S(1)} copy-done((bf16[576,512]{1,0:T(8,128)(2,1)S(1)}, bf16[576,512]{1,0:T(8,128)(2,1)}, u32[]{:S(2)}) %copy-start) | copy-done | bytes 589848
  1.7 0.0 copy-start.1
  1.7 1.1 %copy-done.1 = bf16[576,512]{1,0:T(8,128)(2,1)S(1)} copy-done((bf16[576,512]{1,0:T(8,128)(2,1)S(1)}, bf16[576,512]{1,0:T(8,128)(2,1)}, u32[]{:S(2)}) %copy-start.1) | copy-done | bytes 589848
  2.8 0.0 copy-start.2
  2.8 0.9 %copy-done.2 = bf16[1,32,2048]{2,1,0:T(8,128)(2,1)S(1)} copy-done((bf16[1,32,2048]{2,1,0:T(8,128)(2,1)S(1)}, bf16[1,32,2048]{2,1,0:T(8,128)(2,1)}, u32[]{:S(2)}) %copy-start.2) | copy-done | bytes 131096
  3.7 0.0 copy-start.3
  3.7 0.9 %copy-done.3 = bf16[1,32,2048]{2,1,0:T(8,128)(2,1)S(1)} copy-done((bf16[1,32,2048]{2,1,0:T(8,128)(2,1)S(1)}, bf16[1,32,2048]{2,1,0:T(8,128)(2,1)}, u32[]{:S(2)}) %copy-start.3) | copy-done | bytes 131096
  4.6 0.0 copy-start.4
  4.6 0.8 %copy-done.4 = bf16[1,32,512]{2,1,0:T(8,128)(2,1)S(1)} copy-done((bf16[1,32,512]{2,1,0:T(8,128)(2,1)S(1)}, bf16[1,32,512]{2,1,0:T(8,128)(2,1)}, u32[]{:S(2)}) %copy-start.4) | copy-done | bytes 32792
  5.3 0.0 copy-start.5
  5.3 0.8 %copy-done.5 = bf16[1,32,512]{2,1,0:T(8,128)(2,1)S(1)} copy-done((bf16[1,32,512]{2,1,0:T(8,128)(2,1)S(1)}, bf16[1,32,512]{2,1,0:T(8,128)(2,1)}, u32[]{:S(2)}) %copy-start.5) | copy-done | bytes 32792
  6.1 0.0 copy-start.6
  6.1 0.7 %copy-done.6 = s32[16]{0:T(128)S(1)} copy-done((s32[16]{0:T(128)S(1)}, s32[16]{0:T(128)}, u32[]{:S(2)}) %copy-start.6) | copy-done | bytes 88
  6.7 0.0 copy-start.7
  6.7 0.7 %copy-done.7 = s32[16]{0:T(128)S(1)} copy-done((s32[16]{0:T(128)S(1)}, s32[16]{0:T(128)}, u32[]{:S(2)}) %copy-start.7) | copy-done | bytes 88
  7.4 0.0 copy-start.8
  7.4 0.7 %copy-done.8 = s32[1,32]{1,0:T(1,128)S(1)} copy-done((s32[1,32]{1,0:T(1,128)S(1)}, s32[1,32]{1,0:T(1,128)}, u32[]{:S(2)}) %copy-start.8) | copy-done | bytes 152
  8.1 0.0 copy-start.9
  8.1 0.7 %copy-done.9 = s32[1,8]{1,0:T(1,128)S(1)} copy-done((s32[1,8]{1,0:T(1,128)S(1)}, s32[1,8]{1,0:T(1,128)}, u32[]{:S(2)}) %copy-start.9) | copy-done | bytes 56
  8.7 21.3 %tree_attention.1 = (bf16[1,32,2048]{2,1,0:T(8,128)(2,1)S(1)}, bf16[576,512]{1,0:T(8,128)(2,1)S(1)}, bf16[576,512]{1,0:T(8,128)(2,1)S(1)}) custom-call(s32[16]{0:T(128)S(1)} %copy-done.6, s32[16]{0:T(128)S(1)} %copy-done.7, s32[1,32]{1,0:T(1,128)S(1)} %copy-done.8, s32[1,8]{1,0:T(1,128)S(1)} %copy-done.9, bf16[1,32,2048]{2,1,0:T(8,128)(2,1)S(1)} %copy-done.2, ...), custom_call_target="tpu_custom_call" | custom-call | tf_op jit(solution)/shard_map/tree_attention/pallas_call | solution.py:375
  30.0 0.7 %copy.17 = bf16[1,32,2048]{2,1,0:T(8,128)(2,1)} copy(bf16[1,32,2048]{2,1,0:T(8,128)(2,1)S(1)} %get-tuple-element.6) | data formatting | bytes 262144
  30.7 0.8 %copy.18 = bf16[576,512]{1,0:T(8,128)(2,1)} copy(bf16[576,512]{1,0:T(8,128)(2,1)S(1)} %get-tuple-element.7) | data formatting | bytes 1179648
  31.5 0.8 %copy.19 = bf16[576,512]{1,0:T(8,128)(2,1)} copy(bf16[576,512]{1,0:T(8,128)(2,1)S(1)} %get-tuple-element.8) | data formatting | bytes 1179648
Async XLA Ops:
  0.6 1.1 %copy-start = (bf16[576,512]{1,0:T(8,128)(2,1)S(1)}, bf16[576,512]{1,0:T(8,128)(2,1)}, u32[]{:S(2)}) copy-start(bf16[576,512]{1,0:T(8,128)(2,1)} %ck_hbm.1) | copy-start | bytes 1769476
  1.7 1.1 %copy-start.1 = (bf16[576,512]{1,0:T(8,128)(2,1)S(1)}, bf16[576,512]{1,0:T(8,128)(2,1)}, u32[]{:S(2)}) copy-start(bf16[576,512]{1,0:T(8,128)(2,1)} %cv_hbm.1) | copy-start | bytes 1769476
  2.8 0.9 %copy-start.2 = (bf16[1,32,2048]{2,1,0:T(8,128)(2,1)S(1)}, bf16[1,32,2048]{2,1,0:T(8,128)(2,1)}, u32[]{:S(2)}) copy-start(bf16[1,32,2048]{2,1,0:T(8,128)(2,1)} %q_hbm.1) | copy-start | bytes 393220
  3.7 0.9 %copy-start.3 = (bf16[1,32,2048]{2,1,0:T(8,128)(2,1)S(1)}, bf16[1,32,2048]{2,1,0:T(8,128)(2,1)}, u32[]{:S(2)}) copy-start(bf16[1,32,2048]{2,1,0:T(8,128)(2,1)} %res_hbm.1) | copy-start | bytes 393220
  4.6 0.8 %copy-start.4 = (bf16[1,32,512]{2,1,0:T(8,128)(2,1)S(1)}, bf16[1,32,512]{2,1,0:T(8,128)(2,1)}, u32[]{:S(2)}) copy-start(bf16[1,32,512]{2,1,0:T(8,128)(2,1)} %tk_hbm.1) | copy-start | bytes 98308
  5.3 0.8 %copy-start.5 = (bf16[1,32,512]{2,1,0:T(8,128)(2,1)S(1)}, bf16[1,32,512]{2,1,0:T(8,128)(2,1)}, u32[]{:S(2)}) copy-start(bf16[1,32,512]{2,1,0:T(8,128)(2,1)} %tv_hbm.1) | copy-start | bytes 98308
  6.1 0.7 %copy-start.6 = (s32[16]{0:T(128)S(1)}, s32[16]{0:T(128)}, u32[]{:S(2)}) copy-start(s32[16]{0:T(128)} %len_ref.1) | copy-start | bytes 196
  6.7 0.7 %copy-start.7 = (s32[16]{0:T(128)S(1)}, s32[16]{0:T(128)}, u32[]{:S(2)}) copy-start(s32[16]{0:T(128)} %acc_len_ref.1) | copy-start | bytes 196
  7.4 0.7 %copy-start.8 = (s32[1,32]{1,0:T(1,128)S(1)}, s32[1,32]{1,0:T(1,128)}, u32[]{:S(2)}) copy-start(s32[1,32]{1,0:T(1,128)} %parents_ref.1) | copy-start | bytes 388
  8.1 0.7 %copy-start.9 = (s32[1,8]{1,0:T(1,128)S(1)}, s32[1,8]{1,0:T(1,128)}, u32[]{:S(2)}) copy-start(s32[1,8]{1,0:T(1,128)} %accept_ref.1) | copy-start | bytes 100

commit v2 on v1

--- a/solution.py
+++ b/solution.py
@@ -15,15 +15,16 @@
 NEG = -1e30
 FLOOR = -1e29
 TAIL = 16
+CUTS = 4
 MESH = pl.DeviceIdType.MESH
 
 
 def kernel(
     n_tp,
-    len_ref,
-    acc_len_ref,
-    parents_ref,
-    accept_ref,
+    len_hbm,
+    acc_len_hbm,
+    parents_hbm,
+    accept_hbm,
     q_hbm,
     tk_hbm,
     tv_hbm,
@@ -34,6 +35,10 @@
     mixed_ref,
     nk_hbm,
     nv_hbm,
+    len_ref,
+    acc_len_ref,
+    parents_ref,
+    accept_ref,
     kbuf,
     vbuf,
     vt,
@@ -85,6 +90,11 @@
     def peer_of(d):
         return (low + d % 2) % 2 + 2 * ((high + d // 2) % 2)
 
+    barrier = pltpu.get_barrier_semaphore()
+    for d in range(1, GROUP):
+        pl.semaphore_signal(barrier, inc=1, device_id=(base + peer_of(d), tp), device_id_type=MESH)
+    for d in range(1, n_tp):
+        pl.semaphore_signal(barrier, inc=1, device_id=(seq, (tp + d) % n_tp), device_id_type=MESH)
     locals_ = [
         pltpu.make_async_copy(tk_hbm.at[0], kbuf.at[pl.ds(positions, TREE)], loc_sem.at[0]),
         pltpu.make_async_copy(tv_hbm.at[0], vbuf.at[pl.ds(positions, TREE)], loc_sem.at[1]),
@@ -92,15 +102,14 @@
         pltpu.make_async_copy(ck_hbm, kbuf.at[pl.ds(0, positions)], loc_sem.at[3]),
         pltpu.make_async_copy(cv_hbm, vbuf.at[pl.ds(0, positions)], loc_sem.at[4]),
         pltpu.make_async_copy(res_hbm.at[0], resbuf, loc_sem.at[5]),
+        pltpu.make_async_copy(len_hbm, len_ref, loc_sem.at[6]),
+        pltpu.make_async_copy(acc_len_hbm, acc_len_ref, loc_sem.at[7]),
+        pltpu.make_async_copy(parents_hbm, parents_ref, loc_sem.at[8]),
+        pltpu.make_async_copy(accept_hbm, accept_ref, loc_sem.at[9]),
     ]
     for c in locals_:
         c.start()
 
-    barrier = pltpu.get_barrier_semaphore()
-    for d in range(1, GROUP):
-        pl.semaphore_signal(barrier, inc=1, device_id=(base + peer_of(d), tp), device_id_type=MESH)
-    for d in range(1, n_tp):
-        pl.semaphore_signal(barrier, inc=1, device_id=(seq, (tp + d) % n_tp), device_id_type=MESH)
     pl.semaphore_wait(barrier, GROUP - 1 + n_tp - 1)
 
     def q_copy(d, k):
@@ -148,10 +157,13 @@
         return pltpu.make_async_copy(w_hbm.at[rows_k], wbuf.at[rows_k], w_sem.at[k])
 
     for k in range(kv):
-        for d in (1, 2, 3):
+        for d in (3, 1, 2):
             q_copy(d, k).start()
     for k in range(kv):
         w_copy(k).start()
+
+    for i in (6, 7, 8, 9):
+        locals_[i].wait()
 
     lens = [len_ref[base + r] for r in range(GROUP)]
     begins = []
@@ -242,24 +254,26 @@
         )
         return carry
 
-    lax.fori_loop(0, kv, own_step, 0)
 
     tail_row = lax.broadcasted_iota(i32, (TAIL, lanes), 0)
 
     def peer_step(k, carry):
         for d in (1, 2, 3):
             q_copy(d, k).wait_recv()
-            out, top, total = attend(qbuf[d - 1, k], k, d)
+        found = [attend(qbuf[d - 1, k], k, d) for d in (1, 2, 3)]
+        for d, (out, top, total) in zip((1, 2, 3), found):
             psend[d - 1, k, pl.ds(0, HD), :] = out.astype(jnp.bfloat16)
             main = total.astype(jnp.bfloat16).astype(jnp.float32)
             tail = jnp.where(
                 tail_row == 0, top, jnp.where(tail_row == 1, main, total - main)
             )
             psend[d - 1, k, pl.ds(HD, TAIL), :] = tail.astype(jnp.bfloat16)
+        for d in (3, 1, 2):
             p_copy(d, k).start()
         return carry
 
     lax.fori_loop(0, kv, peer_step, 0)
+    lax.fori_loop(0, kv, own_step, 0)
 
     for d in range(1, GROUP):
         r_copy(d).wait_recv()
@@ -357,6 +371,21 @@
         t_copy(d).wait_send()
 
 
+def write_out(a, b, c, a_out, b_out, c_out, sem):
+    copies = []
+    part = b.shape[0] // CUTS
+    for src, dst in ((b, b_out), (c, c_out)):
+        for i in range(CUTS):
+            rows = pl.ds(i * part, part)
+            copies.append((src.at[rows], dst.at[rows]))
+    copies.append((a, a_out))
+    copies = [pltpu.make_async_copy(x, y, sem.at[i]) for i, (x, y) in enumerate(copies)]
+    for copy in copies:
+        copy.start()
+    for copy in copies:
+        copy.wait()
+
+
 def on_device(n_tp, queries, tree_keys, tree_values, cache_keys, cache_values, residual, out_weight, cache_len, parents, accept_rows, accept_len):
     positions, channels = cache_keys.shape
     kv = channels // HD
@@ -369,19 +398,23 @@
     peers = GROUP - 1
     vmem = pltpu.VMEM
     dma = pltpu.SemaphoreType.DMA
-    hbm = pl.BlockSpec(memory_space=pl.ANY)
-    smem = pl.BlockSpec(memory_space=pltpu.SMEM)
+    hbm = pl.BlockSpec(memory_space=pltpu.HBM)
     local = pl.BlockSpec(memory_space=pltpu.VMEM)
-    return pl.pallas_call(
+    results = (
+        jax.ShapeDtypeStruct(residual.shape, bf16),
+        jax.ShapeDtypeStruct(cache_keys.shape, bf16),
+        jax.ShapeDtypeStruct(cache_values.shape, bf16),
+    )
+    made = pl.pallas_call(
         functools.partial(kernel, n_tp),
-        out_shape=(
-            jax.ShapeDtypeStruct(residual.shape, bf16),
-            jax.ShapeDtypeStruct(cache_keys.shape, bf16),
-            jax.ShapeDtypeStruct(cache_values.shape, bf16),
-        ),
-        in_specs=[smem, smem, local, local] + [hbm] * 7,
+        out_shape=results,
+        in_specs=[hbm] * 11,
         out_specs=(local, hbm, hbm),
         scratch_shapes=[
+            pltpu.SMEM(cache_len.shape, jnp.int32),
+            pltpu.SMEM(accept_len.shape, jnp.int32),
+            vmem(parents.shape, jnp.int32),
+            vmem(accept_rows.shape, jnp.int32),
             vmem((span, channels), bf16),
             vmem((span, channels), bf16),
             vmem((kv, HD, span), bf16),
@@ -402,7 +435,7 @@
             vmem((TREE, w_loc), bf16),
             vmem((positions, channels), bf16),
             vmem((positions, channels), bf16),
-            dma((6,)),
+            dma((10,)),
             dma((kv,)),
             dma((2,)),
             dma((peers, kv)),
@@ -415,10 +448,19 @@
             dma((max(n_tp - 1, 1),)),
         ],
         compiler_params=pltpu.CompilerParams(
-            collective_id=0, has_side_effects=True, vmem_limit_bytes=48 * 1024 * 1024
+            collective_id=0, has_side_effects=True, vmem_limit_bytes=62 * 1024 * 1024
         ),
         name="tree_attention",
     )(cache_len, accept_len, parents, accept_rows, queries, tree_keys, tree_values, cache_keys, cache_values, residual, out_weight)
+    return pl.pallas_call(
+        write_out,
+        out_shape=results,
+        in_specs=[hbm] * 3,
+        out_specs=(hbm, hbm, hbm),
+        scratch_shapes=[dma((2 * CUTS + 1,))],
+        compiler_params=pltpu.CompilerParams(vmem_limit_bytes=62 * 1024 * 1024),
+        name="write_out",
+    )(*made)
 
 
 def solution(mesh):

time: 32.7 us -> 62.5 us (1.91)
  Pallas kernels: 21.3 us -> 61.7 us
  local copies, waits for them, and re-layouts: 10.3 us -> 0 us
    pallas_call x1 -> x2, Pallas kernels: 21.3 us -> 61.7 us  [the longest x1 40.9 us: on_device(): pl.pallas_call(write_out, out_shape=results, in_specs=[hbm] * 3, out_spec...]
    unnamed x23 -> x0, local copies, waits for them, and re-layouts: 10.3 us -> none
where the time goes in v2:
time: 62.5 us; the launch traced here: 62.4 us
  Pallas kernels  61.7 us (99%)
  between operations  0.64 us (1%)
    pallas_call x1, Pallas kernels, on_device(): pl.pallas_call(write_out, out_shape=results, in_specs=[hbm] * 3, out_spec...  40.9 us
    pallas_call x1, Pallas kernels, on_device(): pl.pallas_call(functools.partial(kernel, n_tp), out_shape=results, in_spe...  20.8 us

profile of v2, /device:TPU:0, one launch (start us, length us, event | category | flops | bytes accessed | tf_op | source)
XLA Modules:
  0.0 62.4 jit_solution(4412436141710363803)
XLA Ops:
  0.6 20.8 %tree_attention.1 = (bf16[1,32,2048]{2,1,0:T(8,128)(2,1)}, bf16[576,512]{1,0:T(8,128)(2,1)}, bf16[576,512]{1,0:T(8,128)(2,1)}) custom-call(s32[16]{0:T(128)} %len_hbm.1, s32[16]{0:T(128)} %acc_len_hbm.1, s32[1,32]{1,0:T(1,128)} %parents_hbm.1, s32[1,8]{1,0:T(1,128)} %accept_hbm.1, bf16[1,32,2048]{2,1,0:T(8,128)(2,1)} %q_hbm.1, bf16[1,32,512]{2,1,0:T(8,128)(2,1)} %tk_hbm.1, ...), custom_call_target="tpu_custom_call" | custom-call | tf_op jit(solution)/shard_map/tree_attention/pallas_call | solution.py:408
  21.5 40.9 %write_out.1 = (bf16[1,32,2048]{2,1,0:T(8,128)(2,1)}, bf16[576,512]{1,0:T(8,128)(2,1)}, bf16[576,512]{1,0:T(8,128)(2,1)}) custom-call(bf16[1,32,2048]{2,1,0:T(8,128)(2,1)} %get-tuple-element.6.a, bf16[576,512]{1,0:T(8,128)(2,1)} %get-tuple-element.7.b, bf16[576,512]{1,0:T(8,128)(2,1)} %get-tuple-element.8.c), custom_call_target="tpu_custom_call" | custom-call | tf_op jit(solution)/shard_map/write_out/pallas_call | solution.py:455

commit v3 on v2

--- a/solution.py
+++ b/solution.py
@@ -15,7 +15,7 @@
 NEG = -1e30
 FLOOR = -1e29
 TAIL = 16
-CUTS = 4
+CUTS = 3
 MESH = pl.DeviceIdType.MESH
 
 
@@ -122,6 +122,16 @@
             device_id_type=MESH,
         )
 
+    def forward(k, via):
+        return pltpu.make_async_remote_copy(
+            src_ref=qbuf.at[2 - via, k],
+            dst_ref=qbuf.at[2, k],
+            send_sem=q_ss.at[2, k],
+            recv_sem=q_rs.at[2, k],
+            device_id=(base + peer_of(via), tp),
+            device_id_type=MESH,
+        )
+
     def p_copy(d, k):
         return pltpu.make_async_remote_copy(
             src_ref=psend.at[d - 1, k],
@@ -157,7 +167,7 @@
         return pltpu.make_async_copy(w_hbm.at[rows_k], wbuf.at[rows_k], w_sem.at[k])
 
     for k in range(kv):
-        for d in (3, 1, 2):
+        for d in (1, 2):
             q_copy(d, k).start()
     for k in range(kv):
         w_copy(k).start()
@@ -257,22 +267,30 @@
 
     tail_row = lax.broadcasted_iota(i32, (TAIL, lanes), 0)
 
-    def peer_step(k, carry):
-        for d in (1, 2, 3):
-            q_copy(d, k).wait_recv()
-        found = [attend(qbuf[d - 1, k], k, d) for d in (1, 2, 3)]
-        for d, (out, top, total) in zip((1, 2, 3), found):
+    def answer(k, ds):
+        found = [attend(qbuf[d - 1, k], k, d) for d in ds]
+        for d, (out, top, total) in zip(ds, found):
             psend[d - 1, k, pl.ds(0, HD), :] = out.astype(jnp.bfloat16)
             main = total.astype(jnp.bfloat16).astype(jnp.float32)
             tail = jnp.where(
                 tail_row == 0, top, jnp.where(tail_row == 1, main, total - main)
             )
             psend[d - 1, k, pl.ds(HD, TAIL), :] = tail.astype(jnp.bfloat16)
-        for d in (3, 1, 2):
+        for d in ds:
             p_copy(d, k).start()
+
+    for k in range(kv):
+        q_copy(1, k).wait_recv()
+        q_copy(2, k).wait_recv()
+        forward(k, 1 + k % 2).start()
+        answer(k, (1, 2))
+
+    def far_step(k, carry):
+        q_copy(3, k).wait_recv()
+        answer(k, (3,))
         return carry
 
-    lax.fori_loop(0, kv, peer_step, 0)
+    lax.fori_loop(0, kv, far_step, 0)
     lax.fori_loop(0, kv, own_step, 0)
 
     for d in range(1, GROUP):
@@ -365,24 +383,30 @@
     for d in range(1, GROUP):
         r_copy(d).wait_send()
         for k in range(kv):
-            q_copy(d, k).wait_send()
+            if d < 3:
+                q_copy(d, k).wait_send()
+            else:
+                forward(k, 1 + k % 2).wait_send()
             p_copy(d, k).wait_send()
     for d in range(1, n_tp):
         t_copy(d).wait_send()
 
 
-def write_out(a, b, c, a_out, b_out, c_out, sem):
-    copies = []
+def write_out(a, b, c, a_out, b_out, c_out, a_mem, b_mem, c_mem, in_sem, sem):
+    hops = [(a, a_mem, a_out)]
     part = b.shape[0] // CUTS
-    for src, dst in ((b, b_out), (c, c_out)):
+    for src, mem, dst in ((b, b_mem, b_out), (c, c_mem, c_out)):
         for i in range(CUTS):
             rows = pl.ds(i * part, part)
-            copies.append((src.at[rows], dst.at[rows]))
-    copies.append((a, a_out))
-    copies = [pltpu.make_async_copy(x, y, sem.at[i]) for i, (x, y) in enumerate(copies)]
-    for copy in copies:
+            hops.append((src.at[rows], mem.at[rows], dst.at[rows]))
+    loads = [pltpu.make_async_copy(x, m, in_sem.at[i]) for i, (x, m, y) in enumerate(hops)]
+    stores = [pltpu.make_async_copy(m, y, sem.at[i]) for i, (x, m, y) in enumerate(hops)]
+    for copy in loads:
         copy.start()
-    for copy in copies:
+    for load, store in zip(loads, stores):
+        load.wait()
+        store.start()
+    for copy in stores:
         copy.wait()
 
 
@@ -457,7 +481,13 @@
         out_shape=results,
         in_specs=[hbm] * 3,
         out_specs=(hbm, hbm, hbm),
-        scratch_shapes=[dma((2 * CUTS + 1,))],
+        scratch_shapes=[
+            vmem(residual.shape, bf16),
+            vmem(cache_keys.shape, bf16),
+            vmem(cache_values.shape, bf16),
+            dma((2 * CUTS + 1,)),
+            dma((2 * CUTS + 1,)),
+        ],
         compiler_params=pltpu.CompilerParams(vmem_limit_bytes=62 * 1024 * 1024),
         name="write_out",
     )(*made)

time: 62.5 us -> 25 us (0.40)
  Pallas kernels: 61.7 us -> 24.2 us
    pallas_call x1, Pallas kernels: 40.9 us -> 2.18 us  [on_device(): pl.pallas_call(write_out, out_shape=results, in_specs=[hbm] * 3, out_spec...]
    pallas_call x1, Pallas kernels: 20.8 us -> 22 us  [on_device(): pl.pallas_call(functools.partial(kernel, n_tp), out_shape=results, in_spe...]
where the time goes in v3:
time: 25 us; the launch traced here: 24.9 us
  Pallas kernels  24.2 us (97%)
  between operations  0.64 us (3%)
    pallas_call x1, Pallas kernels, on_device(): pl.pallas_call(functools.partial(kernel, n_tp), out_shape=results, in_spe...  22 us
    pallas_call x1, Pallas kernels, on_device(): pl.pallas_call(write_out, out_shape=results, in_specs=[hbm] * 3, out_spec...  2.18 us

profile of v3, /device:TPU:0, one launch (start us, length us, event | category | flops | bytes accessed | tf_op | source)
XLA Modules:
  0.0 24.9 jit_solution(5971927613404750982)
XLA Ops:
  0.6 22.0 %tree_attention.1 = (bf16[1,32,2048]{2,1,0:T(8,128)(2,1)}, bf16[576,512]{1,0:T(8,128)(2,1)}, bf16[576,512]{1,0:T(8,128)(2,1)}) custom-call(s32[16]{0:T(128)} %len_hbm.1, s32[16]{0:T(128)} %acc_len_hbm.1, s32[1,32]{1,0:T(1,128)} %parents_hbm.1, s32[1,8]{1,0:T(1,128)} %accept_hbm.1, bf16[1,32,2048]{2,1,0:T(8,128)(2,1)} %q_hbm.1, bf16[1,32,512]{2,1,0:T(8,128)(2,1)} %tk_hbm.1, ...), custom_call_target="tpu_custom_call" | custom-call | tf_op jit(solution)/shard_map/tree_attention/pallas_call | solution.py:432
  22.7 2.2 %write_out.1 = (bf16[1,32,2048]{2,1,0:T(8,128)(2,1)}, bf16[576,512]{1,0:T(8,128)(2,1)}, bf16[576,512]{1,0:T(8,128)(2,1)}) custom-call(bf16[1,32,2048]{2,1,0:T(8,128)(2,1)} %get-tuple-element.6.a, bf16[576,512]{1,0:T(8,128)(2,1)} %get-tuple-element.7.b, bf16[576,512]{1,0:T(8,128)(2,1)} %get-tuple-element.8.c), custom_call_target="tpu_custom_call" | custom-call | tf_op jit(solution)/shard_map/write_out/pallas_call | solution.py:479

commit v4 on v3

--- a/solution.py
+++ b/solution.py
@@ -122,16 +122,6 @@
             device_id_type=MESH,
         )
 
-    def forward(k, via):
-        return pltpu.make_async_remote_copy(
-            src_ref=qbuf.at[2 - via, k],
-            dst_ref=qbuf.at[2, k],
-            send_sem=q_ss.at[2, k],
-            recv_sem=q_rs.at[2, k],
-            device_id=(base + peer_of(via), tp),
-            device_id_type=MESH,
-        )
-
     def p_copy(d, k):
         return pltpu.make_async_remote_copy(
             src_ref=psend.at[d - 1, k],
@@ -167,7 +157,7 @@
         return pltpu.make_async_copy(w_hbm.at[rows_k], wbuf.at[rows_k], w_sem.at[k])
 
     for k in range(kv):
-        for d in (1, 2):
+        for d in (3, 1, 2):
             q_copy(d, k).start()
     for k in range(kv):
         w_copy(k).start()
@@ -189,8 +179,8 @@
             first = jnp.where(peer == r, begins[r], first)
             size = jnp.where(peer == r, lens[r], size)
         inside = (place >= first) & (place < first + size)
-        bias[d, pl.ds(0, positions), :] = jnp.where(inside, 0.0, NEG)
-        bias[d, pl.ds(positions, span - positions), :] = jnp.full(
+        bias[pl.ds(0, positions), d * lanes : (d + 1) * lanes] = jnp.where(inside, 0.0, NEG)
+        bias[pl.ds(positions, span - positions), d * lanes : (d + 1) * lanes] = jnp.full(
             (span - positions, lanes), NEG, jnp.float32
         )
 
@@ -209,7 +199,7 @@
         0.0,
     ).astype(jnp.bfloat16)
     linked = jnp.dot(reach.astype(jnp.bfloat16), spread, preferred_element_type=jnp.float32)
-    bias[0, pl.ds(positions, TREE), :] = jnp.where(linked > 0.5, 0.0, NEG)
+    bias[pl.ds(positions, TREE), 0:lanes] = jnp.where(linked > 0.5, 0.0, NEG)
 
     if span > used:
         kbuf[pl.ds(used, span - used), :] = jnp.zeros((span - used, channels), jnp.bfloat16)
@@ -240,58 +230,44 @@
     for k in range(kv):
         vt[k] = vbuf[:, k * HD : (k + 1) * HD].astype(jnp.float32).T.astype(jnp.bfloat16)
 
-    def attend(queries, k, which):
+    tail_row = lax.broadcasted_iota(i32, (TAIL, lanes), 0)
+
+    def attend(k, carry):
+        for d in (1, 2, 3):
+            q_copy(d, k).wait_recv()
+        blocks = [qown[:, pl.ds(pl.multiple_of(k * qk, qk), qk)]]
+        blocks += [qbuf[d - 1, k] for d in (1, 2, 3)]
         stacked = jnp.concatenate(
-            [queries[:, g * HD : (g + 1) * HD] for g in range(sharing)], axis=0
+            [q[:, g * HD : (g + 1) * HD] for q in blocks for g in range(sharing)], axis=0
         )
         keys = kbuf[:, pl.ds(pl.multiple_of(k * HD, HD), HD)]
         scores = lax.dot_general(
             keys, stacked, (((1,), (1,)), ((), ())), preferred_element_type=jnp.float32
         )
-        scores = scores + bias[which]
+        scores = scores + bias[...]
         top = jnp.maximum(jnp.max(scores, axis=0, keepdims=True), FLOOR)
         top = top.astype(jnp.bfloat16).astype(jnp.float32)
         raised = jnp.exp2((scores - top) * scale)
         total = jnp.sum(raised, axis=0, keepdims=True)
         out = jnp.dot(vt[k], raised.astype(jnp.bfloat16), preferred_element_type=jnp.float32)
-        return out, top, total
-
-    def own_step(k, carry):
-        out, top, total = attend(qown[:, pl.ds(pl.multiple_of(k * qk, qk), qk)], k, 0)
-        own_o[k] = out
-        own_s[k] = jnp.concatenate(
-            [top, total, jnp.zeros((6, lanes), jnp.float32)], axis=0
-        )
-        return carry
-
-
-    tail_row = lax.broadcasted_iota(i32, (TAIL, lanes), 0)
-
-    def answer(k, ds):
-        found = [attend(qbuf[d - 1, k], k, d) for d in ds]
-        for d, (out, top, total) in zip(ds, found):
-            psend[d - 1, k, pl.ds(0, HD), :] = out.astype(jnp.bfloat16)
-            main = total.astype(jnp.bfloat16).astype(jnp.float32)
+        for d in (3, 1, 2):
+            mine = slice(d * lanes, (d + 1) * lanes)
+            psend[d - 1, k, pl.ds(0, HD), :] = out[:, mine].astype(jnp.bfloat16)
+            whole = total[:, mine]
+            main = whole.astype(jnp.bfloat16).astype(jnp.float32)
             tail = jnp.where(
-                tail_row == 0, top, jnp.where(tail_row == 1, main, total - main)
+                tail_row == 0, top[:, mine], jnp.where(tail_row == 1, main, whole - main)
             )
             psend[d - 1, k, pl.ds(HD, TAIL), :] = tail.astype(jnp.bfloat16)
-        for d in ds:
+        for d in (3, 1, 2):
             p_copy(d, k).start()
-
-    for k in range(kv):
-        q_copy(1, k).wait_recv()
-        q_copy(2, k).wait_recv()
-        forward(k, 1 + k % 2).start()
-        answer(k, (1, 2))
-
-    def far_step(k, carry):
-        q_copy(3, k).wait_recv()
-        answer(k, (3,))
+        own_o[k] = out[:, :lanes]
+        own_s[k] = jnp.concatenate(
+            [top[:, :lanes], total[:, :lanes], jnp.zeros((6, lanes), jnp.float32)], axis=0
+        )
         return carry
 
-    lax.fori_loop(0, kv, far_step, 0)
-    lax.fori_loop(0, kv, own_step, 0)
+    lax.fori_loop(0, kv, attend, 0)
 
     for d in range(1, GROUP):
         r_copy(d).wait_recv()
@@ -383,10 +359,7 @@
     for d in range(1, GROUP):
         r_copy(d).wait_send()
         for k in range(kv):
-            if d < 3:
-                q_copy(d, k).wait_send()
-            else:
-                forward(k, 1 + k % 2).wait_send()
+            q_copy(d, k).wait_send()
             p_copy(d, k).wait_send()
     for d in range(1, n_tp):
         t_copy(d).wait_send()
@@ -444,7 +417,7 @@
             vmem((kv, HD, span), bf16),
             vmem((TREE, q_width), bf16),
             vmem((peers, kv, TREE, qk), bf16),
-            vmem((GROUP, span, lanes), f32),
+            vmem((span, GROUP * lanes), f32),
             vmem((kv, HD, lanes), f32),
             vmem((kv, 8, lanes), f32),
             vmem((peers, kv, HD + TAIL, lanes), bf16),

time: 25 us -> 23.8 us (0.952)
  Pallas kernels: 24.2 us -> 23 us
    pallas_call x1, Pallas kernels: 22 us -> 20.8 us  [on_device(): pl.pallas_call(functools.partial(kernel, n_tp), out_shape=results, in_spe...]
where the time goes in v4:
time: 23.8 us; the launch traced here: 23.6 us
  Pallas kernels  23 us (97%)
  between operations  0.64 us (3%)
    pallas_call x1, Pallas kernels, on_device(): pl.pallas_call(functools.partial(kernel, n_tp), out_shape=results, in_spe...  20.8 us
    pallas_call x1, Pallas kernels, on_device(): pl.pallas_call(write_out, out_shape=results, in_specs=[hbm] * 3, out_spec...  2.18 us

profile of v4, /device:TPU:0, one launch (start us, length us, event | category | flops | bytes accessed | tf_op | source)
XLA Modules:
  0.0 23.6 jit_solution(2158878627803713948)
XLA Ops:
  0.6 20.8 %tree_attention.1 = (bf16[1,32,2048]{2,1,0:T(8,128)(2,1)}, bf16[576,512]{1,0:T(8,128)(2,1)}, bf16[576,512]{1,0:T(8,128)(2,1)}) custom-call(s32[16]{0:T(128)} %len_hbm.1, s32[16]{0:T(128)} %acc_len_hbm.1, s32[1,32]{1,0:T(1,128)} %parents_hbm.1, s32[1,8]{1,0:T(1,128)} %accept_hbm.1, bf16[1,32,2048]{2,1,0:T(8,128)(2,1)} %q_hbm.1, bf16[1,32,512]{2,1,0:T(8,128)(2,1)} %tk_hbm.1, ...), custom_call_target="tpu_custom_call" | custom-call | tf_op jit(solution)/shard_map/tree_attention/pallas_call | solution.py:405
  21.5 2.2 %write_out.1 = (bf16[1,32,2048]{2,1,0:T(8,128)(2,1)}, bf16[576,512]{1,0:T(8,128)(2,1)}, bf16[576,512]{1,0:T(8,128)(2,1)}) custom-call(bf16[1,32,2048]{2,1,0:T(8,128)(2,1)} %get-tuple-element.6.a, bf16[576,512]{1,0:T(8,128)(2,1)} %get-tuple-element.7.b, bf16[576,512]{1,0:T(8,128)(2,1)} %get-tuple-element.8.c), custom_call_target="tpu_custom_call" | custom-call | tf_op jit(solution)/shard_map/write_out/pallas_call | solution.py:452

commit v5 on v4

--- a/solution.py
+++ b/solution.py
@@ -390,7 +390,7 @@
     qk = q_width // kv
     lanes = qk // HD * TREE
     w_loc = residual.shape[2]
-    span = -(-(positions + TREE) // 128) * 128
+    span = positions + TREE
     bf16, f32 = jnp.bfloat16, jnp.float32
     peers = GROUP - 1
     vmem = pltpu.VMEM

time: 23.8 us -> 23.8 us (level)
  no operation moved by 1% of the time
where the time goes in v5:
time: 23.8 us; the launch traced here: 23.6 us
  Pallas kernels  23 us (97%)
  between operations  0.64 us (3%)
    pallas_call x1, Pallas kernels, on_device(): pl.pallas_call(functools.partial(kernel, n_tp), out_shape=results, in_spe...  20.8 us
    pallas_call x1, Pallas kernels, on_device(): pl.pallas_call(write_out, out_shape=results, in_specs=[hbm] * 3, out_spec...  2.18 us

profile of v5, /device:TPU:0, one launch (start us, length us, event | category | flops | bytes accessed | tf_op | source)
XLA Modules:
  0.0 23.6 jit_solution(8831925095689745010)
XLA Ops:
  0.6 20.8 %tree_attention.1 = (bf16[1,32,2048]{2,1,0:T(8,128)(2,1)}, bf16[576,512]{1,0:T(8,128)(2,1)}, bf16[576,512]{1,0:T(8,128)(2,1)}) custom-call(s32[16]{0:T(128)} %len_hbm.1, s32[16]{0:T(128)} %acc_len_hbm.1, s32[1,32]{1,0:T(1,128)} %parents_hbm.1, s32[1,8]{1,0:T(1,128)} %accept_hbm.1, bf16[1,32,2048]{2,1,0:T(8,128)(2,1)} %q_hbm.1, bf16[1,32,512]{2,1,0:T(8,128)(2,1)} %tk_hbm.1, ...), custom_call_target="tpu_custom_call" | custom-call | tf_op jit(solution)/shard_map/tree_attention/pallas_call | solution.py:405
  21.5 2.2 %write_out.1 = (bf16[1,32,2048]{2,1,0:T(8,128)(2,1)}, bf16[576,512]{1,0:T(8,128)(2,1)}, bf16[576,512]{1,0:T(8,128)(2,1)}) custom-call(bf16[1,32,2048]{2,1,0:T(8,128)(2,1)} %get-tuple-element.6.a, bf16[576,512]{1,0:T(8,128)(2,1)} %get-tuple-element.7.b, bf16[576,512]{1,0:T(8,128)(2,1)} %get-tuple-element.8.c), custom_call_target="tpu_custom_call" | custom-call | tf_op jit(solution)/shard_map/write_out/pallas_call | solution.py:452
